TPU v7x, 1024 devices: a whole 4x8x16 slice. The times are simulated.
1024 devices in a mesh: patch: 64 (over z_hi, x, y), ens: 16 (over z_lo, core).
Axes of the slice: x: 4, y: 8, z: 16 (z_hi: 2, z_lo: 8; z = z_hi * 8 + z_lo), core: 2. Of those that a mesh axis runs over, the one named last changes fastest.
Arguments:
- pred: bfloat16 [16, 8192, 128], P('ens', 'patch'), may hold values from -6 to 6
- target: bfloat16 [8192, 128], P('patch'), may hold values from -6 to 6
- h1: bfloat16 [16, 8192, 1024], P('ens', 'patch'), may hold values from -6 to 6
- w1: bfloat16 [1024, 1024], replicated, may hold values from -0.1875 to 0.1875
- w2: bfloat16 [1024, 128], replicated, may hold values from -0.5 to 0.5
- neighbours: int32 [64, 256, 6], P('patch'), may hold values from 0 to 255, as said below
- rotations: int32 [64, 256, 6], P('patch'), may hold values from 0 to 7, as said below
Outputs:
- grad_h1: bfloat16 [16, 8192, 1024], P('ens', 'patch')
Inputs may be any that keep to these rules, and one draw needn't show every extreme that they name: Row l of patch p's table lists the neighbours of vertex p * 128 - 2 * 32 + l as window rows; every neighbour lies 1 to 32 vertices away in vertex order, and column 0 exactly 32. All tables agree on every vertex that they share. Rows of vertices outside the mesh, and neighbours outside the window, name the row itself. `rotations`: tables of all patches agree on every vertex that they share.
All inputs are finite; a program needn't handle non-finite values.
Results may differ from a plain program's by a relative error of at most 0.023.
Values may be sent and summed in bfloat16 or wider, within the bound.
A program may use at most 32 MiB of HBM per device.

v0:
```python
import math

import jax
import jax.numpy as jnp
from jax import lax
from jax.sharding import PartitionSpec as P

K = 6
H = 32


angle_step = 2.0 * math.pi / 8.0


def with_halo(cells, sides, width):
    for axis, dim in sides:
        count = lax.axis_size(axis)
        ends = count - 1
        head = lax.slice_in_dim(cells, 0, width, axis=dim)
        tail = lax.slice_in_dim(cells, cells.shape[dim] - width, cells.shape[dim], axis=dim)
        cells = jnp.concatenate(
            [
                lax.ppermute(tail, axis, [(i, (i + 1) % count) for i in range(ends)]),
                cells,
                lax.ppermute(head, axis, [((i + 1) % count, i) for i in range(ends)]),
            ],
            axis=dim,
        )
    return cells


def rotate_pairs(block, cosines, sines):
    half_width = block.shape[-1] // 2
    real_part = block[:, :half_width]
    imag_part = block[:, half_width:]
    return jnp.concatenate(
        [
            cosines[:, None] * real_part - sines[:, None] * imag_part,
            sines[:, None] * real_part + cosines[:, None] * imag_part,
        ],
        axis=1,
    )


def spread_rows(values, links, cosines, sines, window):
    slots = jnp.arange(window, dtype=jnp.int32)[:, None]
    cos_map = jnp.zeros((window, values.shape[0]), jnp.float32)
    sin_map = jnp.zeros((window, values.shape[0]), jnp.float32)
    for column in range(links.shape[1]):
        hits = (links[:, column][None, :] == slots).astype(jnp.float32)
        cos_map = cos_map + hits * cosines[:, column][None, :]
        sin_map = sin_map + hits * sines[:, column][None, :]
    half_width = values.shape[1] // 2
    real_part = values[:, :half_width]
    imag_part = values[:, half_width:]
    high = lax.Precision.HIGHEST
    out_real = jnp.dot(cos_map, real_part, precision=high) + jnp.dot(
        sin_map, imag_part, precision=high
    )
    out_imag = jnp.dot(cos_map, imag_part, precision=high) - jnp.dot(
        sin_map, real_part, precision=high
    )
    return jnp.concatenate([out_real, out_imag], axis=1)


def per_device(pred, target, h1, w1, w2, neighbours, rotations):
    members = lax.axis_size("ens")
    core_rows = h1.shape[1]
    channels = h1.shape[2]
    regrouped = lax.all_to_all(pred, "ens", split_axis=1, concat_axis=0, tiled=True).astype(
        jnp.float32
    )
    share_rows = regrouped.shape[1]
    offset = lax.axis_index("ens") * share_rows
    observed = lax.dynamic_slice_in_dim(target, offset, share_rows, 0).astype(jnp.float32)
    sign_total = jnp.sum(jnp.sign(regrouped[:, None] - regrouped[None, :]), axis=1)
    loss_grad = (jnp.sign(regrouped - observed[None]) - sign_total / (members - 1)).astype(
        jnp.bfloat16
    )
    member_grad = lax.all_to_all(loss_grad, "ens", split_axis=0, concat_axis=1, tiled=True)[0]
    link_table = neighbours[0]
    angles = rotations[0].astype(jnp.float32) * angle_step
    cosines = jnp.cos(angles)
    sine_part = jnp.sin(angles)
    window = link_table.shape[0]
    depth = 2 * H
    base = 2 * H - depth
    first = H
    span = core_rows + 2 * H
    hidden_ext = with_halo(h1[0], (("patch", 0),), depth)
    summed_rows = jnp.zeros((span, channels), jnp.float32)
    for column in range(K):
        summed_rows = summed_rows + rotate_pairs(
            hidden_ext[link_table[first : first + span, column] - base].astype(jnp.float32),
            cosines[first : first + span, column],
            sine_part[first : first + span, column],
        )
    pre_act = jnp.dot(summed_rows.astype(jnp.bfloat16), w1, preferred_element_type=jnp.float32)
    grad_ext = with_halo(member_grad, (("patch", 0),), depth)
    grad_agg = lax.dot_general(
        grad_ext, w2, (((1,), (1,)), ((), ())), preferred_element_type=jnp.float32
    )
    grad_mid = spread_rows(grad_agg, link_table, cosines, sine_part, window)
    sigmoid_val = jax.nn.sigmoid(pre_act)
    act_grad = (
        grad_mid[first : first + span] * sigmoid_val * (1.0 + pre_act * (1.0 - sigmoid_val))
    ).astype(jnp.bfloat16)
    back_agg = lax.dot_general(
        act_grad, w1, (((1,), (1,)), ((), ())), preferred_element_type=jnp.float32
    )
    spread = spread_rows(
        back_agg,
        link_table[first : first + span],
        cosines[first : first + span],
        sine_part[first : first + span],
        window,
    )
    result = grad_mid[2 * H : 2 * H + core_rows] + spread[2 * H : 2 * H + core_rows]
    return result.astype(jnp.bfloat16)[None]


def solution(mesh):
    return jax.shard_map(
        per_device,
        mesh=mesh,
        in_specs=(
            P("ens", "patch", None),
            P("patch", None),
            P("ens", "patch", None),
            P(),
            P(),
            P("patch", None, None),
            P("patch", None, None),
        ),
        out_specs=P("ens", "patch", None),
        check_vma=False,
    )
```

profile of v0, /device:TPU:832, one launch (start us, length us, event | category | flops | bytes accessed | tf_op | source)
XLA Modules:
  0.0 117.4 jit_solution(13720049592620191624)
XLA Ops:
  0.0 1.0 copy.21
  1.0 0.5 broadcast.108
  1.5 0.8 reduce
  2.3 0.6 reshape.117
  2.9 9.9 %all-to-all-start = ((bf16[16,2,512]{2,1,0:T(2,128)(2,1)}), bf16[16,2,512]{2,1,0:T(2,128)(2,1)S(1)}, u32[]{:S(2)}, u32[]{:S(2)}) async-start(bf16[16,2,512]{2,1,0:T(2,128)(2,1)} %reshape.117), calls=%async_computation | async-start | bytes 65536 | tf_op jit(solution)/shard_map/all_to_all | solution.py:70
  12.9 1.0 slice_bitcast_fusion.1
  13.9 7.8 %collective-permute-start.3 = (bf16[64,1024]{1,0:T(8,128)(2,1)S(1)}, bf16[64,1024]{1,0:T(8,128)(2,1)S(1)}, u32[]{:S(2)}, u32[]{:S(2)}) collective-permute-start(bf16[64,1024]{1,0:T(8,128)(2,1)S(1)} %get-tuple-element.18), channel_id=1, source_target_pairs={{16,0},{32,16},{48,32},{64,48},{80,64},{96,80},{112,96},{128,112},... | collective-permute-start | bytes 393224 | tf_op jit(solution)/shard_map/ppermute | solution.py:25
  21.7 1.9 %collective-permute-start.2 = (bf16[64,1024]{1,0:T(8,128)(2,1)S(1)}, bf16[64,1024]{1,0:T(8,128)(2,1)S(1)}, u32[]{:S(2)}, u32[]{:S(2)}) collective-permute-start(bf16[64,1024]{1,0:T(8,128)(2,1)S(1)} %get-tuple-element.17), channel_id=1, source_target_pairs={{0,16},{16,32},{32,48},{48,64},{64,80},{80,96},{96,112},{112,128},... | collective-permute-start | bytes 393224 | tf_op jit(solution)/shard_map/ppermute | solution.py:23
  23.6 0.7 copy.20
  24.3 0.6 fusion.56
  24.9 0.1 compare_select_fusion
  25.0 0.9 fusion.38
  25.9 0.6 fusion.55
  26.5 0.1 fusion.54
  26.6 0.6 fusion.57
  27.2 0.1 fusion.53
  27.3 0.8 slice.265
  28.2 0.6 fusion.52
  28.8 0.7 dynamic-slice_convert_fusion
  29.5 0.0 all-to-all-done
  29.5 0.1 bitcast_convert_fusion
  29.6 0.3 sign_reduce_fusion
  29.9 0.6 subtract_convert_fusion
  30.6 9.9 %all-to-all-start.1 = ((bf16[16,8,128]{2,1,0:T(8,128)(2,1)}), bf16[16,8,128]{2,1,0:T(8,128)(2,1)S(1)}, u32[]{:S(2)}, u32[]{:S(2)}) async-start(bf16[16,8,128]{2,1,0:T(8,128)(2,1)} %subtract_convert_fusion), calls=%async_computation.1 | async-start | bytes 65536 | tf_op jit(solution)/shard_map/all_to_all | solution.py:80
  40.5 0.0 collective-permute-done.3
  40.5 4.3 %collective-permute-done.2 = bf16[64,1024]{1,0:T(8,128)(2,1)S(1)} collective-permute-done((bf16[64,1024]{1,0:T(8,128)(2,1)S(1)}, bf16[64,1024]{1,0:T(8,128)(2,1)S(1)}, u32[]{:S(2)}, u32[]{:S(2)}) %collective-permute-start.2) | collective-permute-done | bytes 131104 | tf_op jit(solution)/shard_map/ppermute | solution.py:23
  44.7 1.0 pad_maximum_fusion.2
  45.7 1.8 %gather_fusion = bf16[192,1024]{1,0:T(8,128)(2,1)} fusion(bf16[256,1024]{1,0:T(8,128)(2,1)S(1)} %pad_maximum_fusion.2, s32[1024]{0:T(1024)S(1)} %pad_clamp_fusion.5), kind=kCustom, calls=%fused_computation | custom fusion | bytes 787200 | tf_op jit(solution)/shard_map/gather | solution.py:94
  47.5 1.1 convert_element_type.68
  48.6 1.8 %gather_fusion.1 = bf16[192,1024]{1,0:T(8,128)(2,1)} fusion(bf16[256,1024]{1,0:T(8,128)(2,1)S(1)} %pad_maximum_fusion.2, s32[1024]{0:T(1024)S(1)} %pad_clamp_fusion.4), kind=kCustom, calls=%fused_computation.1 | custom fusion | bytes 787200 | tf_op jit(solution)/shard_map/gather | solution.py:94
  50.3 2.0 %convert_element_type.69 = f32[192,1024]{1,0:T(8,128)} convert(bf16[192,1024]{1,0:T(8,128)(2,1)} %gather_fusion.1) | non-fusion elementwise | flops 196608 | bytes 1179648 | tf_op jit(solution)/shard_map/convert_element_type | solution.py:94
  52.3 1.8 %gather_fusion.2 = bf16[192,1024]{1,0:T(8,128)(2,1)} fusion(bf16[256,1024]{1,0:T(8,128)(2,1)S(1)} %pad_maximum_fusion.2, s32[1024]{0:T(1024)S(1)} %pad_clamp_fusion.3), kind=kCustom, calls=%fused_computation.2 | custom fusion | bytes 787200 | tf_op jit(solution)/shard_map/gather | solution.py:94
  54.1 2.0 %convert_element_type.70 = f32[192,1024]{1,0:T(8,128)} convert(bf16[192,1024]{1,0:T(8,128)(2,1)} %gather_fusion.2) | non-fusion elementwise | flops 196608 | bytes 1179648 | tf_op jit(solution)/shard_map/convert_element_type | solution.py:94
  56.0 1.8 %gather_fusion.3 = bf16[192,1024]{1,0:T(8,128)(2,1)} fusion(bf16[256,1024]{1,0:T(8,128)(2,1)S(1)} %pad_maximum_fusion.2, s32[1024]{0:T(1024)S(1)} %pad_clamp_fusion.2), kind=kCustom, calls=%fused_computation.3 | custom fusion | bytes 787200 | tf_op jit(solution)/shard_map/gather | solution.py:94
  57.8 2.0 %convert_element_type.71 = f32[192,1024]{1,0:T(8,128)} convert(bf16[192,1024]{1,0:T(8,128)(2,1)} %gather_fusion.3) | non-fusion elementwise | flops 196608 | bytes 1179648 | tf_op jit(solution)/shard_map/convert_element_type | solution.py:94
  59.8 1.8 %gather_fusion.4 = bf16[192,1024]{1,0:T(8,128)(2,1)} fusion(bf16[256,1024]{1,0:T(8,128)(2,1)S(1)} %pad_maximum_fusion.2, s32[1024]{0:T(1024)S(1)} %pad_clamp_fusion.1), kind=kCustom, calls=%fused_computation.4 | custom fusion | bytes 787200 | tf_op jit(solution)/shard_map/gather | solution.py:94
  61.5 1.2 %convert_element_type.72 = f32[192,1024]{1,0:T(8,128)S(1)} convert(bf16[192,1024]{1,0:T(8,128)(2,1)} %gather_fusion.4) | non-fusion elementwise | flops 196608 | bytes 1179648 | tf_op jit(solution)/shard_map/convert_element_type | solution.py:94
  62.8 1.1 multiply_subtract_fusion.5
  63.8 1.0 multiply_subtract_fusion.4
  64.9 1.0 multiply_subtract_fusion.3
  65.9 1.0 multiply_subtract_fusion.2
  67.0 1.1 multiply_subtract_fusion.1
  68.0 1.0 gather_fusion.5
  69.1 0.0 copy-start.20
  69.1 0.0 copy-start.34
  69.1 0.0 copy-start.35
  69.1 0.1 convert_element_type.73
  69.2 0.0 all-to-all-done.1
  69.2 12.6 %collective-permute-start.1 = (bf16[64,128]{1,0:T(8,128)(2,1)S(1)}, bf16[64,128]{1,0:T(8,128)(2,1)S(1)}, u32[]{:S(2)}, u32[]{:S(2)}) collective-permute-start(bf16[64,128]{1,0:T(8,128)(2,1)S(1)} %get-tuple-element.20), channel_id=1, source_target_pairs={{16,0},{32,16},{48,32},{64,48},{80,64},{96,80},{112,96},{128,112},... | collective-permute-start | bytes 49160 | tf_op jit(solution)/shard_map/ppermute | solution.py:25
  81.8 2.1 %collective-permute-start = (bf16[64,128]{1,0:T(8,128)(2,1)S(1)}, bf16[64,128]{1,0:T(8,128)(2,1)S(1)}, u32[]{:S(2)}, u32[]{:S(2)}) collective-permute-start(bf16[64,128]{1,0:T(8,128)(2,1)S(1)} %get-tuple-element.19), channel_id=1, source_target_pairs={{0,16},{16,32},{32,48},{48,64},{64,80},{80,96},{96,112},{112,128},... | collective-permute-start | bytes 49160 | tf_op jit(solution)/shard_map/ppermute | solution.py:23
  84.0 1.0 multiply_subtract_fusion
  85.0 0.0 collective-permute-done.1
  85.0 15.4 %collective-permute-done = bf16[64,128]{1,0:T(8,128)(2,1)S(1)} collective-permute-done((bf16[64,128]{1,0:T(8,128)(2,1)S(1)}, bf16[64,128]{1,0:T(8,128)(2,1)S(1)}, u32[]{:S(2)}, u32[]{:S(2)}) %collective-permute-start) | collective-permute-done | bytes 16416 | tf_op jit(solution)/shard_map/ppermute | solution.py:23
  100.4 1.2 %fusion.32 = f32[256,1024]{1,0:T(8,128)S(1)} fusion(bf16[1024,128]{1,0:T(8,128)(2,1)} %param.11, bf16[64,128]{1,0:T(8,128)(2,1)S(1)} %collective-permute-done.1, bf16[128,128]{1,0:T(8,128)(2,1)S(1)} %bitcast.76, bf16[64,128]{1,0:T(8,128)(2,1)S(1)} %collective-permute-done), kind=kOutput, calls=%fused_computation.73 | convolution fusion | flops 67305472 | bytes 1376256 | tf_op jit(solution)/shard_map/dot_general | solution.py:100
  101.8 0.8 fusion.11
  102.6 0.8 fusion.15
  103.5 1.5 %convolution_subtract_fusion.1 = f32[256,512]{1,0:T(8,128)S(1)} fusion(f32[256,512]{1,0:T(8,128)S(1)} %fusion.11, f32[256,1024]{1,0:T(8,128)S(1)} %fusion.32, f32[256]{0:T(256)S(1)} %bitcast.173, f32[256]{0:T(256)S(1)} %bitcast.175, f32[256]{0:T(256)S(1)} %bitcast.177, f32[256]{0:T(256)S(1)} %bitcast.179, f32[256]{0:T(256)S(1)} %bitcast.181, ...), kind=kOutput, calls=%fused_computation.8 | convolution fusion | flops 403898368 | bytes 1585152 | tf_op jit(solution)/shard_map/dot_general | solution.py:60
  105.1 1.5 %convolution_add_fusion.1 = f32[256,512]{1,0:T(8,128)S(1)} fusion(f32[256,512]{1,0:T(8,128)S(1)} %fusion.15, f32[256,1024]{1,0:T(8,128)S(1)} %fusion.32, f32[256]{0:T(256)S(1)} %bitcast.174, f32[256]{0:T(256)S(1)} %bitcast.176, f32[256]{0:T(256)S(1)} %bitcast.178, f32[256]{0:T(256)S(1)} %bitcast.180, f32[256]{0:T(256)S(1)} %bitcast.182, ...), kind=kOutput, calls=%fused_computation.9 | convolution fusion | flops 403898368 | bytes 1585152 | tf_op jit(solution)/shard_map/dot_general | solution.py:57
  106.6 4.6 %fusion.17 = f32[192,1024]{1,0:T(8,128)} fusion(bf16[1024,1024]{1,0:T(8,128)(2,1)S(1)} %copy-done, f32[256,512]{1,0:T(8,128)S(1)} %convolution_subtract_fusion.1, f32[256,512]{1,0:T(8,128)S(1)} %convolution_add_fusion.1, f32[192,512]{1,0:T(8,128)} %get-tuple-element.16, f32[192,512]{1,0:T(8,128)S(1)} %copy-done.4, f32[192,512]{1,0:T(8,128)} %get-tuple-element.14, ...), kind=kOutput, calls=%fused_computation.46 | convolution fusion | flops 809631744 | bytes 8650752 | tf_op jit(solution)/shard_map/dot_general | solution.py:108
  111.2 1.9 %fusion.25 = f32[256,512]{1,0:T(8,128)S(1)} fusion(f32[192,1024]{1,0:T(8,128)} %fusion.17, f32[192]{0:T(256)} %bitcast.100, s32[192]{0:T(256)} %bitcast.151, f32[192]{0:T(256)} %bitcast.103, s32[192]{0:T(256)} %bitcast.155, f32[192]{0:T(256)} %bitcast.106, s32[192]{0:T(256)} %bitcast.159, f32[192]{0:T(256)} %bitcast.109, s32[192]{0:T(256)} %bitcast.163, ...), kind=kOutput, calls=%fused_computation.48 | convolution fusion | flops 302825472 | bytes 929792 | tf_op jit(solution)/shard_map/dot_general | solution.py:60
  113.1 1.8 %fusion.29 = f32[256,512]{1,0:T(8,128)S(1)} fusion(f32[192,1024]{1,0:T(8,128)} %fusion.17, f32[192]{0:T(256)} %bitcast.101, s32[192]{0:T(256)} %bitcast.152, f32[192]{0:T(256)} %bitcast.104, s32[192]{0:T(256)} %bitcast.156, f32[192]{0:T(256)} %bitcast.107, s32[192]{0:T(256)} %bitcast.160, f32[192]{0:T(256)} %bitcast.110, s32[192]{0:T(256)} %bitcast.164, ...), kind=kOutput, calls=%fused_computation.52 | convolution fusion | flops 302825472 | bytes 929792 | tf_op jit(solution)/shard_map/dot_general | solution.py:57
  115.1 0.8 convolution_subtract_fusion
  115.9 0.8 convolution_add_fusion
  116.7 0.8 fusion.31
  (89 shorter events, 0.2 us)
Async XLA Ops:
  0.0 106.6 %copy-start = (bf16[1024,1024]{1,0:T(8,128)(2,1)S(1)}, bf16[1024,1024]{1,0:T(8,128)(2,1)}, u32[]{:S(2)}) copy-start(bf16[1024,1024]{1,0:T(8,128)(2,1)} %param.10) | copy-start | bytes 6291460
  2.9 26.5 %all-to-all-start = ((bf16[16,2,512]{2,1,0:T(2,128)(2,1)}), bf16[16,2,512]{2,1,0:T(2,128)(2,1)S(1)}, u32[]{:S(2)}, u32[]{:S(2)}) async-start(bf16[16,2,512]{2,1,0:T(2,128)(2,1)} %reshape.117), calls=%async_computation | async-start | bytes 65536 | tf_op jit(solution)/shard_map/all_to_all | solution.py:70
  13.9 26.6 %collective-permute-start.3 = (bf16[64,1024]{1,0:T(8,128)(2,1)S(1)}, bf16[64,1024]{1,0:T(8,128)(2,1)S(1)}, u32[]{:S(2)}, u32[]{:S(2)}) collective-permute-start(bf16[64,1024]{1,0:T(8,128)(2,1)S(1)} %get-tuple-element.18), channel_id=1, source_target_pairs={{16,0},{32,16},{48,32},{64,48},{80,64},{96,80},{112,96},{128,112},... | collective-permute-start | bytes 393224 | tf_op jit(solution)/shard_map/ppermute | solution.py:25
  21.7 23.1 %collective-permute-start.2 = (bf16[64,1024]{1,0:T(8,128)(2,1)S(1)}, bf16[64,1024]{1,0:T(8,128)(2,1)S(1)}, u32[]{:S(2)}, u32[]{:S(2)}) collective-permute-start(bf16[64,1024]{1,0:T(8,128)(2,1)S(1)} %get-tuple-element.17), channel_id=1, source_target_pairs={{0,16},{16,32},{32,48},{48,64},{64,80},{80,96},{96,112},{112,128},... | collective-permute-start | bytes 393224 | tf_op jit(solution)/shard_map/ppermute | solution.py:23
  24.9 77.7 %copy-start.15 = (s32[256,1]{0,1:T(1,128)}, s32[256,1]{0,1:T(1,128)S(1)}, u32[]{:S(2)}) copy-start(s32[256,1]{0,1:T(1,128)S(1)} %get-tuple-element.51) | copy-start | bytes 3076
  24.9 77.7 %copy-start.16 = (s32[256,1]{0,1:T(1,128)}, s32[256,1]{0,1:T(1,128)S(1)}, u32[]{:S(2)}) copy-start(s32[256,1]{0,1:T(1,128)S(1)} %get-tuple-element.52) | copy-start | bytes 3076
  24.9 77.7 %copy-start.17 = (s32[256,1]{0,1:T(1,128)}, s32[256,1]{0,1:T(1,128)S(1)}, u32[]{:S(2)}) copy-start(s32[256,1]{0,1:T(1,128)S(1)} %get-tuple-element.53) | copy-start | bytes 3076
  24.9 77.7 %copy-start.18 = (s32[256,1]{0,1:T(1,128)}, s32[256,1]{0,1:T(1,128)S(1)}, u32[]{:S(2)}) copy-start(s32[256,1]{0,1:T(1,128)S(1)} %get-tuple-element.54) | copy-start | bytes 3076
  24.9 77.7 %copy-start.19 = (s32[256,1]{0,1:T(1,128)}, s32[256,1]{0,1:T(1,128)S(1)}, u32[]{:S(2)}) copy-start(s32[256,1]{0,1:T(1,128)S(1)} %get-tuple-element.55) | copy-start | bytes 3076
  26.6 36.1 %copy-start.7 = (f32[192,1]{0,1:T(1,128)}, f32[192,1]{0,1:T(1,128)S(1)}, u32[]{:S(2)}) copy-start(f32[192,1]{0,1:T(1,128)S(1)} %get-tuple-element.38) | copy-start | bytes 2308
  26.6 37.2 %copy-start.5 = (f32[192,1]{0,1:T(1,128)}, f32[192,1]{0,1:T(1,128)S(1)}, u32[]{:S(2)}) copy-start(f32[192,1]{0,1:T(1,128)S(1)} %get-tuple-element.37) | copy-start | bytes 2308
  27.3 35.5 %copy-start.14 = (f32[192,1]{0,1:T(1,128)}, f32[192,1]{0,1:T(1,128)S(1)}, u32[]{:S(2)}) copy-start(f32[192,1]{0,1:T(1,128)S(1)} %get-tuple-element.32) | copy-start | bytes 2308
  27.3 36.5 %copy-start.13 = (f32[192,1]{0,1:T(1,128)}, f32[192,1]{0,1:T(1,128)S(1)}, u32[]{:S(2)}) copy-start(f32[192,1]{0,1:T(1,128)S(1)} %get-tuple-element.31) | copy-start | bytes 2308
  27.3 37.6 %copy-start.12 = (f32[192,1]{0,1:T(1,128)}, f32[192,1]{0,1:T(1,128)S(1)}, u32[]{:S(2)}) copy-start(f32[192,1]{0,1:T(1,128)S(1)} %get-tuple-element.30) | copy-start | bytes 2308
  27.3 38.6 %copy-start.11 = (f32[192,1]{0,1:T(1,128)}, f32[192,1]{0,1:T(1,128)S(1)}, u32[]{:S(2)}) copy-start(f32[192,1]{0,1:T(1,128)S(1)} %get-tuple-element.29) | copy-start | bytes 2308
  27.3 39.6 %copy-start.10 = (f32[192,1]{0,1:T(1,128)}, f32[192,1]{0,1:T(1,128)S(1)}, u32[]{:S(2)}) copy-start(f32[192,1]{0,1:T(1,128)S(1)} %get-tuple-element.28) | copy-start | bytes 2308
  27.3 56.6 %copy-start.9 = (f32[192,1]{0,1:T(1,128)}, f32[192,1]{0,1:T(1,128)S(1)}, u32[]{:S(2)}) copy-start(f32[192,1]{0,1:T(1,128)S(1)} %get-tuple-element.27) | copy-start | bytes 2308
  30.6 38.7 %all-to-all-start.1 = ((bf16[16,8,128]{2,1,0:T(8,128)(2,1)}), bf16[16,8,128]{2,1,0:T(8,128)(2,1)S(1)}, u32[]{:S(2)}, u32[]{:S(2)}) async-start(bf16[16,8,128]{2,1,0:T(8,128)(2,1)} %subtract_convert_fusion), calls=%async_computation.1 | async-start | bytes 65536 | tf_op jit(solution)/shard_map/all_to_all | solution.py:80
  61.5 2.3 %copy-start.1 = (f32[192,1024]{1,0:T(8,128)S(1)}, f32[192,1024]{1,0:T(8,128)}, u32[]{:S(2)}) copy-start(f32[192,1024]{1,0:T(8,128)} %convert_element_type.69) | copy-start | bytes 2359300
  61.5 3.4 %copy-start.2 = (f32[192,1024]{1,0:T(8,128)S(1)}, f32[192,1024]{1,0:T(8,128)}, u32[]{:S(2)}) copy-start(f32[192,1024]{1,0:T(8,128)} %convert_element_type.70) | copy-start | bytes 2359300
  62.7 3.2 %copy-start.3 = (f32[192,1024]{1,0:T(8,128)S(1)}, f32[192,1024]{1,0:T(8,128)}, u32[]{:S(2)}) copy-start(f32[192,1024]{1,0:T(8,128)} %convert_element_type.71) | copy-start | bytes 2359300
  69.1 32.6 %copy-start.20 = (s32[256,1]{0,1:T(1,128)S(1)}, s32[256,1]{0,1:T(1,128)}, u32[]{:S(2)}) copy-start(s32[256,1]{0,1:T(1,128)} %get-tuple-element.56) | copy-start | bytes 3076
  69.1 32.6 %copy-start.34 = (f32[256,1]{0,1:T(1,128)S(1)}, f32[256,1]{0,1:T(1,128)}, u32[]{:S(2)}) copy-start(f32[256,1]{0,1:T(1,128)} %get-tuple-element.57) | copy-start | bytes 3076
  69.1 32.6 %copy-start.35 = (f32[256,1]{0,1:T(1,128)S(1)}, f32[256,1]{0,1:T(1,128)}, u32[]{:S(2)}) copy-start(f32[256,1]{0,1:T(1,128)} %get-tuple-element.58) | copy-start | bytes 3076
  69.1 32.6 %copy-start.36 = (f32[256,1]{0,1:T(1,128)S(1)}, f32[256,1]{0,1:T(1,128)}, u32[]{:S(2)}) copy-start(f32[256,1]{0,1:T(1,128)} %get-tuple-element.59) | copy-start | bytes 3076
  69.1 32.6 %copy-start.37 = (f32[256,1]{0,1:T(1,128)S(1)}, f32[256,1]{0,1:T(1,128)}, u32[]{:S(2)}) copy-start(f32[256,1]{0,1:T(1,128)} %get-tuple-element.60) | copy-start | bytes 3076
  69.1 32.6 %copy-start.38 = (f32[256,1]{0,1:T(1,128)S(1)}, f32[256,1]{0,1:T(1,128)}, u32[]{:S(2)}) copy-start(f32[256,1]{0,1:T(1,128)} %get-tuple-element.61) | copy-start | bytes 3076
  69.1 32.6 %copy-start.39 = (f32[256,1]{0,1:T(1,128)S(1)}, f32[256,1]{0,1:T(1,128)}, u32[]{:S(2)}) copy-start(f32[256,1]{0,1:T(1,128)} %get-tuple-element.62) | copy-start | bytes 3076
  69.2 15.8 %collective-permute-start.1 = (bf16[64,128]{1,0:T(8,128)(2,1)S(1)}, bf16[64,128]{1,0:T(8,128)(2,1)S(1)}, u32[]{:S(2)}, u32[]{:S(2)}) collective-permute-start(bf16[64,128]{1,0:T(8,128)(2,1)S(1)} %get-tuple-element.20), channel_id=1, source_target_pairs={{16,0},{32,16},{48,32},{64,48},{80,64},{96,80},{112,96},{128,112},... | collective-permute-start | bytes 49160 | tf_op jit(solution)/shard_map/ppermute | solution.py:25
  81.8 18.6 %collective-permute-start = (bf16[64,128]{1,0:T(8,128)(2,1)S(1)}, bf16[64,128]{1,0:T(8,128)(2,1)S(1)}, u32[]{:S(2)}, u32[]{:S(2)}) collective-permute-start(bf16[64,128]{1,0:T(8,128)(2,1)S(1)} %get-tuple-element.19), channel_id=1, source_target_pairs={{0,16},{16,32},{32,48},{48,64},{64,80},{80,96},{96,112},{112,128},... | collective-permute-start | bytes 49160 | tf_op jit(solution)/shard_map/ppermute | solution.py:23
  100.4 3.0 %copy-start.21 = (s32[256,1]{0,1:T(1,128)S(1)}, s32[256,1]{0,1:T(1,128)}, u32[]{:S(2)}) copy-start(s32[256,1]{0,1:T(1,128)} %get-tuple-element.56) | copy-start | bytes 3076
  100.4 3.0 %copy-start.28 = (f32[256,1]{0,1:T(1,128)S(1)}, f32[256,1]{0,1:T(1,128)}, u32[]{:S(2)}) copy-start(f32[256,1]{0,1:T(1,128)} %get-tuple-element.45) | copy-start | bytes 3076
  100.4 3.1 %copy-start.29 = (f32[256,1]{0,1:T(1,128)S(1)}, f32[256,1]{0,1:T(1,128)}, u32[]{:S(2)}) copy-start(f32[256,1]{0,1:T(1,128)} %get-tuple-element.46) | copy-start | bytes 3076
  100.4 3.1 %copy-start.30 = (f32[256,1]{0,1:T(1,128)S(1)}, f32[256,1]{0,1:T(1,128)}, u32[]{:S(2)}) copy-start(f32[256,1]{0,1:T(1,128)} %get-tuple-element.47) | copy-start | bytes 3076
  100.4 3.1 %copy-start.31 = (f32[256,1]{0,1:T(1,128)S(1)}, f32[256,1]{0,1:T(1,128)}, u32[]{:S(2)}) copy-start(f32[256,1]{0,1:T(1,128)} %get-tuple-element.48) | copy-start | bytes 3076
  100.4 3.1 %copy-start.32 = (f32[256,1]{0,1:T(1,128)S(1)}, f32[256,1]{0,1:T(1,128)}, u32[]{:S(2)}) copy-start(f32[256,1]{0,1:T(1,128)} %get-tuple-element.49) | copy-start | bytes 3076
  100.4 3.1 %copy-start.33 = (f32[256,1]{0,1:T(1,128)S(1)}, f32[256,1]{0,1:T(1,128)}, u32[]{:S(2)}) copy-start(f32[256,1]{0,1:T(1,128)} %get-tuple-element.50) | copy-start | bytes 3076
  103.4 3.1 %copy-start.4 = (f32[192,512]{1,0:T(8,128)S(1)}, f32[192,512]{1,0:T(8,128)}, u32[]{:S(2)}) copy-start(f32[192,512]{1,0:T(8,128)} %get-tuple-element.15) | copy-start | bytes 1179652
  111.2 3.8 %copy-start.6 = (f32[192,1]{0,1:T(1,128)S(1)}, f32[192,1]{0,1:T(1,128)}, u32[]{:S(2)}) copy-start(f32[192,1]{0,1:T(1,128)} %copy-done.5) | copy-start | bytes 2308
  111.2 3.8 %copy-start.8 = (f32[192,1]{0,1:T(1,128)S(1)}, f32[192,1]{0,1:T(1,128)}, u32[]{:S(2)}) copy-start(f32[192,1]{0,1:T(1,128)} %copy-done.7) | copy-start | bytes 2308
  111.2 3.8 %copy-start.22 = (s32[192,1]{0,1:T(1,128)S(1)}, s32[192,1]{0,1:T(1,128)}, u32[]{:S(2)}) copy-start(s32[192,1]{0,1:T(1,128)} %get-tuple-element.21) | copy-start | bytes 2308
  111.2 3.8 %copy-start.23 = (s32[192,1]{0,1:T(1,128)S(1)}, s32[192,1]{0,1:T(1,128)}, u32[]{:S(2)}) copy-start(s32[192,1]{0,1:T(1,128)} %get-tuple-element.22) | copy-start | bytes 2308
  111.2 3.8 %copy-start.24 = (s32[192,1]{0,1:T(1,128)S(1)}, s32[192,1]{0,1:T(1,128)}, u32[]{:S(2)}) copy-start(s32[192,1]{0,1:T(1,128)} %get-tuple-element.23) | copy-start | bytes 2308
  111.2 3.8 %copy-start.25 = (s32[192,1]{0,1:T(1,128)S(1)}, s32[192,1]{0,1:T(1,128)}, u32[]{:S(2)}) copy-start(s32[192,1]{0,1:T(1,128)} %get-tuple-element.24) | copy-start | bytes 2308
  111.2 3.8 %copy-start.26 = (s32[192,1]{0,1:T(1,128)S(1)}, s32[192,1]{0,1:T(1,128)}, u32[]{:S(2)}) copy-start(s32[192,1]{0,1:T(1,128)} %get-tuple-element.25) | copy-start | bytes 2308
  111.2 3.8 %copy-start.27 = (s32[192,1]{0,1:T(1,128)S(1)}, s32[192,1]{0,1:T(1,128)}, u32[]{:S(2)}) copy-start(s32[192,1]{0,1:T(1,128)} %get-tuple-element.26) | copy-start | bytes 2308
  111.2 3.8 %copy-start.40 = (f32[192,1024]{1,0:T(8,128)S(1)}, f32[192,1024]{1,0:T(8,128)}, u32[]{:S(2)}) copy-start(f32[192,1024]{1,0:T(8,128)} %fusion.17) | copy-start | bytes 2359300
where the time goes:
time: 119 us; the launch traced here: 117 us
  starting transfers between devices  44.3 us (37%)
  other arithmetic  19.8 us (17%)
  waiting for transfers between devices  19.7 us (17%)
  local copies, waits for them, and re-layouts  17.1 us (14%)
  matrix products  15.8 us (13%)
    ppermute x2, starting transfers between devices, with_halo(): lax.ppermute(head, axis, [((i + 1) % count, i) for i in range(ends)])  20.4 us
    ppermute x2, waiting for transfers between devices, with_halo(): lax.ppermute(tail, axis, [(i, (i + 1) % count) for i in range(ends)])  19.7 us
    all_to_all x1, starting transfers between devices, per_device(): lax.all_to_all(pred, 'ens', split_axis=1, concat_axis=0, tiled=True)  9.94 us
    all_to_all x1, starting transfers between devices, per_device(): lax.all_to_all(loss_grad, 'ens', split_axis=0, concat_axis=1, tiled=True)[0]  9.92 us
    gather x6, local copies, waits for them, and re-layouts, per_device(): hidden_ext[link_table[first:first + span, column] - base]  9.81 us
    convert_element_type x6, other arithmetic, per_device(): hidden_ext[link_table[first:first + span, column] - base]  8.24 us
    sub x6, other arithmetic, rotate_pairs(): cosines[:, None] * real_part - sines[:, None] * imag_part  6.31 us
    dot_general x1, matrix products, per_device(): lax.dot_general(act_grad, w1, (((1,), (1,)), ((), ())), preferred_element...  4.6 us
  transfers between devices with their start and end apart: 6, of which 2 were waited for; matrix products, arithmetic and copies ran while one was open for 28% of the time, Pallas kernels for 0%

commit v1 on v0

v1 whole, which is shorter than its diff:
```python
import functools

import jax
import jax.numpy as jnp
from jax import lax
from jax.experimental import pallas as pl
from jax.experimental.pallas import tpu as pltpu
from jax.sharding import PartitionSpec as P

K = 6
H = 32
MESH = pl.DeviceIdType.MESH
RELAY_SIDE = "far"


def relay_patch(side, index, half):
    if half < 32:
        return side * half + (half - 1 if side else 0)
    row = index // 2
    odd = lax.rem(index, 2)
    return side * half + 8 * row + (1 + 6 * odd if side else 6 * odd)


def relay_job(side, patch, half):
    if half < 32:
        return patch == (2 * half - 1 if side else 0), 0
    local = patch - side * half
    column = lax.rem(local, 8)
    odd, even = (7, 1) if side else (6, 0)
    mine = (local >= 0) & (local < half) & ((column == odd) | (column == even))
    return mine, 2 * (local // 8) + jnp.where(column == odd, 1, 0)


def turn_table(turns):
    diag = jnp.float32(0.70710678118654752)
    zero = jnp.zeros(turns.shape, jnp.float32)
    one = zero + 1.0

    def cosine(r):
        return jnp.where(
            r == 0,
            one,
            jnp.where(
                (r == 1) | (r == 7),
                zero + diag,
                jnp.where((r == 2) | (r == 6), zero, jnp.where(r == 4, -one, zero - diag)),
            ),
        )

    return cosine(turns), cosine((turns + 6) & 7)


def kernel(
    patches,
    members,
    pred,
    target,
    h1,
    w1,
    w2,
    links,
    turns,
    out,
    hext,
    pin,
    tin,
    gout,
    gext,
    w1v,
    w2v,
    w2c,
    maps,
    tmaps,
    deriv,
    gmid,
    back,
    relay,
    load_sem,
    pin_sem,
    tin_sem,
    pred_send,
    tgt_send,
    g_sem,
    g_send,
    h_recv,
    h_send,
    x_send,
    relay_recv,
    relay_send,
):
    me_p = lax.axis_index("patch")
    me = lax.axis_index("ens")
    half = patches // 2
    share = 256 // members
    quarter = members // 4
    pieces = members // 2
    relays = x_send.shape[0]
    row_cuts = min(4, relays)
    piece_rows, piece_cols = relay.shape
    last = patches - 1
    low, high = me < quarter, me >= members - quarter
    middle = jnp.logical_not(low | high)
    tail_side, head_side = (1, 0) if RELAY_SIDE == "far" else (0, 1)
    tail_relay, tail_index = relay_job(tail_side, me_p, half)
    head_relay, head_index = relay_job(head_side, me_p, half)

    own_h = pltpu.make_async_copy(h1, hext.at[pl.ds(64, 128)], load_sem.at[0])
    own_h.start()
    load_w2 = pltpu.make_async_copy(w2, w2v, load_sem.at[1])
    load_w2.start()
    load_w1 = pltpu.make_async_copy(w1, w1v, load_sem.at[2])
    load_w1.start()

    barrier = pltpu.get_barrier_semaphore()

    def greet(patch, ens):
        pl.semaphore_signal(
            barrier, inc=1, device_id={"patch": patch, "ens": ens}, device_id_type=MESH
        )

    def greet_own(i, carry):
        greet(me_p, lax.rem(me + i, members))
        return carry

    lax.fori_loop(1, members, greet_own, 0)

    @pl.when(low & (me_p > 0))
    def _():
        lax.fori_loop(0, members, lambda i, c: (greet(me_p - 1, i), c)[1], 0)

    @pl.when(high & (me_p < last))
    def _():
        lax.fori_loop(0, members, lambda i, c: (greet(me_p + 1, i), c)[1], 0)

    @pl.when((me_p > 0) & (me_p != half))
    def _():
        greet(me_p - 1, me)

    @pl.when((me_p < last) & (me_p != half - 1))
    def _():
        greet(me_p + 1, me)

    @pl.when(me_p == half)
    def _():
        lax.fori_loop(
            0, relays, lambda i, c: (greet(relay_patch(tail_side, i, half), me), c)[1], 0
        )

    @pl.when(me_p == half - 1)
    def _():
        lax.fori_loop(
            0, relays, lambda i, c: (greet(relay_patch(head_side, i, half), me), c)[1], 0
        )

    @pl.when(tail_relay)
    def _():
        greet(half - 1, me)

    @pl.when(head_relay)
    def _():
        greet(half, me)

    def count(flag, amount):
        return jnp.where(flag, amount, 0)

    partners = (
        (members - 1)
        + count(me_p < last, quarter)
        + count(me_p > 0, quarter)
        + count(me_p < last, count(me_p == half - 1, relays - 1) + 1)
        + count(me_p > 0, count(me_p == half, relays - 1) + 1)
        + count(tail_relay, 1)
        + count(head_relay, 1)
    )
    pl.semaphore_wait(barrier, partners)

    def send_pred(piece, patch, ens, slot):
        return pltpu.make_async_remote_copy(
            src_ref=pred.at[pl.ds(piece * share, share)],
            dst_ref=pin.at[me],
            send_sem=pred_send.at[slot],
            recv_sem=pin_sem,
            device_id={"patch": patch, "ens": ens},
            device_id_type=MESH,
        )

    own_pred = pltpu.make_async_copy(
        pred.at[pl.ds(jnp.where(middle, me - quarter, 0) * share, share)], pin.at[me], pin_sem
    )

    def each_pred(act):
        def across(i, carry):
            piece = lax.rem(me + i, pieces)
            upper = piece >= quarter

            @pl.when(upper & (me_p < last))
            def _():
                act(send_pred(piece, me_p + 1, piece - quarter, pieces + piece))

            @pl.when(jnp.logical_not(upper) & (me_p > 0))
            def _():
                act(send_pred(piece, me_p - 1, members - quarter + piece, pieces + piece))

            @pl.when(piece + quarter != me)
            def _():
                act(send_pred(piece, me_p, piece + quarter, piece))

            return carry

        lax.fori_loop(0, pieces, across, 0)

    each_pred(lambda copy: copy.start())

    def send_target(first, patch):
        return pltpu.make_async_remote_copy(
            src_ref=target.at[pl.ds(first, share)],
            dst_ref=tin,
            send_sem=tgt_send,
            recv_sem=tin_sem,
            device_id={"patch": patch, "ens": me},
            device_id_type=MESH,
        )

    def each_target(act):
        @pl.when(low & (me_p < last))
        def _():
            act(send_target((quarter + jnp.where(low, me, 0)) * share, me_p + 1))

        @pl.when(high & (me_p > 0))
        def _():
            act(send_target(jnp.where(high, me - (members - quarter), 0) * share, me_p - 1))

    each_target(lambda copy: copy.start())

    @pl.when(middle)
    def _():
        own_pred.start()
        pltpu.make_async_copy(
            target.at[pl.ds(jnp.where(middle, me - quarter, 0) * share, share)], tin, tin_sem
        ).start()

    def send_tail():
        return pltpu.make_async_remote_copy(
            src_ref=h1.at[pl.ds(64, 64)],
            dst_ref=hext.at[pl.ds(0, 64)],
            send_sem=h_send.at[0],
            recv_sem=h_recv.at[0],
            device_id={"patch": me_p + 1, "ens": me},
            device_id_type=MESH,
        )

    def send_head():
        return pltpu.make_async_remote_copy(
            src_ref=h1.at[pl.ds(0, 64)],
            dst_ref=hext.at[pl.ds(192, 64)],
            send_sem=h_send.at[1],
            recv_sem=h_recv.at[1],
            device_id={"patch": me_p - 1, "ens": me},
            device_id_type=MESH,
        )

    def cut(ref, index, first):
        row = lax.rem(index, row_cuts) * piece_rows + first
        column = pl.multiple_of((index // row_cuts) * piece_cols, 128)
        return ref.at[pl.ds(pl.multiple_of(row, 16), piece_rows), pl.ds(column, piece_cols)]

    def to_relay(index, first, side):
        return pltpu.make_async_remote_copy(
            src_ref=cut(h1, index, first),
            dst_ref=relay,
            send_sem=x_send.at[index],
            recv_sem=relay_recv,
            device_id={"patch": relay_patch(side, index, half), "ens": me},
            device_id_type=MESH,
        )

    def each_halo(act):
        @pl.when((me_p < last) & (me_p != half - 1))
        def _():
            act(send_tail())

        @pl.when((me_p > 0) & (me_p != half))
        def _():
            act(send_head())

        @pl.when(me_p == half - 1)
        def _():
            lax.fori_loop(0, relays, lambda i, c: (act(to_relay(i, 64, tail_side)), c)[1], 0)

        @pl.when(me_p == half)
        def _():
            lax.fori_loop(0, relays, lambda i, c: (act(to_relay(i, 0, head_side)), c)[1], 0)

    each_halo(lambda copy: copy.start())

    def onward(index, first, patch, slot):
        return pltpu.make_async_remote_copy(
            src_ref=relay,
            dst_ref=cut(hext, index, first),
            send_sem=relay_send,
            recv_sem=h_recv.at[slot],
            device_id={"patch": patch, "ens": me},
            device_id_type=MESH,
        )

    def each_relay(act):
        @pl.when(tail_relay)
        def _():
            act(onward(jnp.where(tail_relay, tail_index, 0), 0, half, 0))

        @pl.when(head_relay)
        def _():
            act(onward(jnp.where(head_relay, head_index, 0), 192, half - 1, 1))

    for first in range(0, 256, 128):
        rows = slice(first, first + 128)
        slots = lax.broadcasted_iota(jnp.int32, (128, 256), 0) + first
        cos_map = jnp.zeros((128, 256), jnp.float32)
        sin_map = jnp.zeros((128, 256), jnp.float32)
        for column in range(K):
            cosine, sine = turn_table(turns[column])
            hit = links[column] == slots
            cos_map += jnp.where(hit, cosine, 0.0)
            sin_map += jnp.where(hit, sine, 0.0)
        tmaps[0, rows] = cos_map.astype(jnp.bfloat16)
        tmaps[1, rows] = sin_map.astype(jnp.bfloat16)
        maps[0, :, rows] = cos_map.T.astype(jnp.bfloat16)
        maps[1, :, rows] = sin_map.T.astype(jnp.bfloat16)

    @pl.when(me_p == 0)
    def _():
        hext[0:64] = jnp.zeros((64, hext.shape[1]), hext.dtype)

    @pl.when(me_p == last)
    def _():
        hext[192:256] = jnp.zeros((64, hext.shape[1]), hext.dtype)

    @pl.when(tail_relay | head_relay)
    def _():
        pltpu.make_async_copy(relay, relay, relay_recv).wait()

    each_relay(lambda copy: copy.start())

    outside = (low & (me_p == 0)) | (high & (me_p == last))

    @pl.when(outside)
    def _():
        pin[...] = jnp.zeros(pin.shape, pin.dtype)
        tin[...] = jnp.zeros(tin.shape, tin.dtype)

    @pl.when(jnp.logical_not(outside))
    def _():
        pltpu.make_async_copy(pin, pin, pin_sem).wait()
        pltpu.make_async_copy(tin, tin, tin_sem).wait()

    def side_of(left, right):
        return jnp.where(left > right, 1.0, jnp.where(left < right, -1.0, 0.0))

    values = pin[...].astype(jnp.float32)
    observed = tin[...].astype(jnp.float32)
    total = jnp.zeros(values.shape, jnp.float32)
    for shift in range(1, members // 2 + 1):
        other = jnp.concatenate([values[shift:], values[:shift]], axis=0)
        side = side_of(values, other)
        total += side
        if shift < members // 2:
            total -= jnp.concatenate([side[members - shift :], side[: members - shift]], axis=0)
    gout[...] = (side_of(values, observed[None]) - total / (members - 1)).astype(jnp.bfloat16)

    def send_grad(i):
        to = lax.rem(me + i, members)
        return pltpu.make_async_remote_copy(
            src_ref=gout.at[to],
            dst_ref=gext.at[me],
            send_sem=g_send.at[i],
            recv_sem=g_sem,
            device_id={"patch": me_p, "ens": to},
            device_id_type=MESH,
        )

    lax.fori_loop(1, members, lambda i, c: (send_grad(i).start(), c)[1], 0)
    pltpu.make_async_copy(gout.at[me], gext.at[me], g_sem).start()

    load_w2.wait()
    w2c[0:512, 0:128] = w2v[0:512]
    w2c[0:512, 128:256] = w2v[512:1024]
    w2c[512:1024, 0:128] = w2v[512:1024]
    w2c[512:1024, 128:256] = -w2v[0:512]

    own_h.wait()

    @pl.when(me_p > 0)
    def _():
        pltpu.make_async_copy(hext.at[pl.ds(0, 64)], hext.at[pl.ds(0, 64)], h_recv.at[0]).wait()

    @pl.when(me_p < last)
    def _():
        pltpu.make_async_copy(
            hext.at[pl.ds(192, 64)], hext.at[pl.ds(192, 64)], h_recv.at[1]
        ).wait()

    features = hext[...]
    by_cos = jnp.dot(maps[0, 32:224], features, preferred_element_type=jnp.float32)
    by_sin = jnp.dot(maps[1, 32:224], features, preferred_element_type=jnp.float32)
    summed = jnp.concatenate(
        [
            (by_cos[:, :512] - by_sin[:, 512:]).astype(jnp.bfloat16),
            (by_sin[:, :512] + by_cos[:, 512:]).astype(jnp.bfloat16),
        ],
        axis=1,
    )
    load_w1.wait()
    pre_act = jnp.dot(summed, w1v[...], preferred_element_type=jnp.float32)
    sigmoid = jax.nn.sigmoid(pre_act)
    deriv[...] = sigmoid * (1.0 + pre_act * (1.0 - sigmoid))
    back[0:32] = jnp.zeros((32, back.shape[1]), back.dtype)
    back[224:256] = jnp.zeros((32, back.shape[1]), back.dtype)

    pltpu.make_async_copy(gext, gext, g_sem).wait()
    grads = gext[...].reshape(256, 128)
    spread_grads = jnp.concatenate(
        [
            jnp.dot(tmaps[0, 32:224], grads, preferred_element_type=jnp.float32),
            jnp.dot(tmaps[1, 32:224], grads, preferred_element_type=jnp.float32),
        ],
        axis=1,
    ).astype(jnp.bfloat16)
    contract_last = (((1,), (1,)), ((), ()))
    gmid[...] = lax.dot_general(
        spread_grads, w2c[...], contract_last, preferred_element_type=jnp.float32
    )
    act_grad = (gmid[...] * deriv[...]).astype(jnp.bfloat16)
    back[32:224] = lax.dot_general(
        act_grad, w1v[...], contract_last, preferred_element_type=jnp.float32
    ).astype(jnp.bfloat16)
    rows_back = back[...]
    by_cos = jnp.dot(tmaps[0, 64:192], rows_back, preferred_element_type=jnp.float32)
    by_sin = jnp.dot(tmaps[1, 64:192], rows_back, preferred_element_type=jnp.float32)
    out[:, :512] = (gmid[32:160, :512] + by_cos[:, :512] + by_sin[:, 512:]).astype(out.dtype)
    out[:, 512:] = (gmid[32:160, 512:] + by_cos[:, 512:] - by_sin[:, :512]).astype(out.dtype)

    each_pred(lambda copy: copy.wait_send())
    each_target(lambda copy: copy.wait_send())
    each_halo(lambda copy: copy.wait_send())
    each_relay(lambda copy: copy.wait_send())
    lax.fori_loop(1, members, lambda i, c: (send_grad(i).wait_send(), c)[1], 0)


def per_device(pred, target, h1, w1, w2, neighbours, rotations):
    members = lax.axis_size("ens")
    patches = lax.axis_size("patch")
    rows, channels = h1.shape[1:]
    share = 256 // members
    relays = 8 if patches >= 64 else 1
    row_cuts = min(4, relays)
    anywhere = pl.BlockSpec(memory_space=pltpu.HBM)
    vmem = pl.BlockSpec(memory_space=pltpu.VMEM)
    dma = pltpu.SemaphoreType.DMA
    bf16 = jnp.bfloat16
    result = pl.pallas_call(
        functools.partial(kernel, patches, members),
        out_shape=jax.ShapeDtypeStruct((rows, channels), bf16),
        in_specs=[anywhere, anywhere, anywhere, anywhere, anywhere, vmem, vmem],
        out_specs=vmem,
        scratch_shapes=[
            pltpu.VMEM((256, channels), bf16),
            pltpu.VMEM((members, share, 128), bf16),
            pltpu.VMEM((share, 128), bf16),
            pltpu.VMEM((members, share, 128), bf16),
            pltpu.VMEM((members, share, 128), bf16),
            pltpu.VMEM((channels, channels), bf16),
            pltpu.VMEM((channels, 128), bf16),
            pltpu.VMEM((channels, 256), bf16),
            pltpu.VMEM((2, 256, 256), bf16),
            pltpu.VMEM((2, 256, 256), bf16),
            pltpu.VMEM((192, channels), jnp.float32),
            pltpu.VMEM((192, channels), jnp.float32),
            pltpu.VMEM((256, channels), bf16),
            pltpu.VMEM((64 // row_cuts, channels * row_cuts // relays), bf16),
            dma((3,)),
            dma(()),
            dma(()),
            dma((members,)),
            dma(()),
            dma(()),
            dma((members,)),
            dma((2,)),
            dma((2,)),
            dma((relays,)),
            dma(()),
            dma(()),
        ],
        compiler_params=pltpu.CompilerParams(
            collective_id=0, has_side_effects=True, vmem_limit_bytes=62 * 2**20
        ),
        name="mesh_backward",
    )(
        pred[0],
        target,
        h1[0],
        w1,
        w2,
        jnp.transpose(neighbours, (2, 0, 1)),
        jnp.transpose(rotations, (2, 0, 1)),
    )
    return result[None]


def solution(mesh):
    return jax.shard_map(
        per_device,
        mesh=mesh,
        in_specs=(
            P("ens", "patch", None),
            P("patch", None),
            P("ens", "patch", None),
            P(),
            P(),
            P("patch", None, None),
            P("patch", None, None),
        ),
        out_specs=P("ens", "patch", None),
        check_vma=False,
    )
```

time: 119 us -> 50.9 us (0.43)
  the two profiles are of different devices: /device:TPU:832 before, /device:TPU:7 now
where the time goes in v1:
time: 50.9 us; the launch traced here: 50.7 us
  Pallas kernels  49.1 us (96%)
  local copies, waits for them, and re-layouts  1.67 us (3%)
    pallas_call x1, Pallas kernels, per_device(): pl.pallas_call(functools.partial(kernel, patches, members), out_shape=jax...  49.1 us
    unnamed x1, local copies, waits for them, and re-layouts  1.67 us

profile of v1, /device:TPU:7, one launch (start us, length us, event | category | flops | bytes accessed | tf_op | source)
XLA Modules:
  0.0 50.7 jit_solution(6120809416444014089)
XLA Ops:
  0.0 49.1 %mesh_backward.1 = bf16[128,1024]{1,0:T(8,128)(2,1)} custom-call(bf16[128,128]{1,0:T(8,128)(2,1)} %bitcast.7, bf16[128,128]{1,0:T(8,128)(2,1)} %target.1, bf16[128,1024]{1,0:T(8,128)(2,1)} %bitcast.6, bf16[1024,1024]{1,0:T(8,128)(2,1)} %w1.1, bf16[1024,128]{1,0:T(8,128)(2,1)} %w2.1, s32[6,1,256]{2,1,0:T(1,128)} %bitcast.8, s32[6,1,256]{2,1,0:T(1,128)} %bitcast.9), custom_call_target="tpu_custom_call" | custom-call | tf_op jit(solution)/shard_map/mesh_backward/pallas_call | solution.py:460
  49.1 1.7 %copy.9 = bf16[1,128,1024]{2,1,0:T(8,128)(2,1)} copy(bf16[1,128,1024]{2,1,0:T(8,128)(2,1)} %bitcast.5) | data formatting | bytes 524288

commit v2 on v1

--- a/solution.py
+++ b/solution.py
@@ -10,7 +10,7 @@
 K = 6
 H = 32
 MESH = pl.DeviceIdType.MESH
-RELAY_SIDE = "far"
+RELAY_SIDE = "near"
 
 
 def relay_patch(side, index, half):
@@ -18,7 +18,7 @@
         return side * half + (half - 1 if side else 0)
     row = index // 2
     odd = lax.rem(index, 2)
-    return side * half + 8 * row + (1 + 6 * odd if side else 6 * odd)
+    return side * half + 8 * row + (2 + 5 * odd if side else 1 + 5 * odd)
 
 
 def relay_job(side, patch, half):
@@ -26,7 +26,7 @@
         return patch == (2 * half - 1 if side else 0), 0
     local = patch - side * half
     column = lax.rem(local, 8)
-    odd, even = (7, 1) if side else (6, 0)
+    odd, even = (7, 2) if side else (6, 1)
     mine = (local >= 0) & (local < half) & ((column == odd) | (column == even))
     return mine, 2 * (local // 8) + jnp.where(column == odd, 1, 0)
 
@@ -87,19 +87,25 @@
     x_send,
     relay_recv,
     relay_send,
+    ready,
 ):
     me_p = lax.axis_index("patch")
     me = lax.axis_index("ens")
     half = patches // 2
-    share = 256 // members
-    quarter = members // 4
-    pieces = members // 2
+    scorers = members // 2
+    share = 256 // scorers
+    pieces = scorers // 2
+    quarter = scorers // 4
+    base = members // 4
     relays = x_send.shape[0]
     row_cuts = min(4, relays)
     piece_rows, piece_cols = relay.shape
     last = patches - 1
-    low, high = me < quarter, me >= members - quarter
-    middle = jnp.logical_not(low | high)
+    place = me - base
+    scorer = (place >= 0) & (place < scorers)
+    low = scorer & (place < quarter)
+    high = scorer & (place >= scorers - quarter)
+    middle = (place >= quarter) & (place < scorers - quarter)
     tail_side, head_side = (1, 0) if RELAY_SIDE == "far" else (0, 1)
     tail_relay, tail_index = relay_job(tail_side, me_p, half)
     head_relay, head_index = relay_job(head_side, me_p, half)
@@ -122,7 +128,9 @@
         greet(me_p, lax.rem(me + i, members))
         return carry
 
-    lax.fori_loop(1, members, greet_own, 0)
+    @pl.when(scorer)
+    def _():
+        lax.fori_loop(1, members, greet_own, 0)
 
     @pl.when(low & (me_p > 0))
     def _():
@@ -164,7 +172,8 @@
         return jnp.where(flag, amount, 0)
 
     partners = (
-        (members - 1)
+        scorers
+        - count(scorer, 1)
         + count(me_p < last, quarter)
         + count(me_p > 0, quarter)
         + count(me_p < last, count(me_p == half - 1, relays - 1) + 1)
@@ -174,19 +183,26 @@
     )
     pl.semaphore_wait(barrier, partners)
 
-    def send_pred(piece, patch, ens, slot):
-        return pltpu.make_async_remote_copy(
-            src_ref=pred.at[pl.ds(piece * share, share)],
+    def tell(i, carry):
+        @pl.when(i != place)
+        def _():
+            pl.semaphore_signal(
+                ready, inc=1, device_id={"patch": me_p, "ens": base + i}, device_id_type=MESH
+            )
+
+        return carry
+
+    lax.fori_loop(0, scorers, tell, 0)
+
+    def send_pred(piece, patch, to, slot):
+        return pltpu.make_async_remote_copy(
+            src_ref=pred.at[pl.ds(pl.multiple_of(piece * share, 16), share)],
             dst_ref=pin.at[me],
             send_sem=pred_send.at[slot],
             recv_sem=pin_sem,
-            device_id={"patch": patch, "ens": ens},
-            device_id_type=MESH,
-        )
-
-    own_pred = pltpu.make_async_copy(
-        pred.at[pl.ds(jnp.where(middle, me - quarter, 0) * share, share)], pin.at[me], pin_sem
-    )
+            device_id={"patch": patch, "ens": base + to},
+            device_id_type=MESH,
+        )
 
     def each_pred(act):
         def across(i, carry):
@@ -199,9 +215,9 @@
 
             @pl.when(jnp.logical_not(upper) & (me_p > 0))
             def _():
-                act(send_pred(piece, me_p - 1, members - quarter + piece, pieces + piece))
-
-            @pl.when(piece + quarter != me)
+                act(send_pred(piece, me_p - 1, scorers - quarter + piece, pieces + piece))
+
+            @pl.when(piece + quarter != place)
             def _():
                 act(send_pred(piece, me_p, piece + quarter, piece))
 
@@ -213,7 +229,7 @@
 
     def send_target(first, patch):
         return pltpu.make_async_remote_copy(
-            src_ref=target.at[pl.ds(first, share)],
+            src_ref=target.at[pl.ds(pl.multiple_of(first, 16), share)],
             dst_ref=tin,
             send_sem=tgt_send,
             recv_sem=tin_sem,
@@ -224,20 +240,19 @@
     def each_target(act):
         @pl.when(low & (me_p < last))
         def _():
-            act(send_target((quarter + jnp.where(low, me, 0)) * share, me_p + 1))
+            act(send_target((quarter + jnp.where(low, place, 0)) * share, me_p + 1))
 
         @pl.when(high & (me_p > 0))
         def _():
-            act(send_target(jnp.where(high, me - (members - quarter), 0) * share, me_p - 1))
+            act(send_target(jnp.where(high, place - (scorers - quarter), 0) * share, me_p - 1))
 
     each_target(lambda copy: copy.start())
 
     @pl.when(middle)
     def _():
-        own_pred.start()
-        pltpu.make_async_copy(
-            target.at[pl.ds(jnp.where(middle, me - quarter, 0) * share, share)], tin, tin_sem
-        ).start()
+        own = pl.ds(pl.multiple_of(jnp.where(middle, place - quarter, 0) * share, 16), share)
+        pltpu.make_async_copy(pred.at[own], pin.at[me], pin_sem).start()
+        pltpu.make_async_copy(target.at[own], tin, tin_sem).start()
 
     def send_tail():
         return pltpu.make_async_remote_copy(
@@ -343,43 +358,55 @@
 
     outside = (low & (me_p == 0)) | (high & (me_p == last))
 
-    @pl.when(outside)
-    def _():
-        pin[...] = jnp.zeros(pin.shape, pin.dtype)
-        tin[...] = jnp.zeros(tin.shape, tin.dtype)
-
-    @pl.when(jnp.logical_not(outside))
-    def _():
-        pltpu.make_async_copy(pin, pin, pin_sem).wait()
-        pltpu.make_async_copy(tin, tin, tin_sem).wait()
-
     def side_of(left, right):
         return jnp.where(left > right, 1.0, jnp.where(left < right, -1.0, 0.0))
 
-    values = pin[...].astype(jnp.float32)
-    observed = tin[...].astype(jnp.float32)
-    total = jnp.zeros(values.shape, jnp.float32)
-    for shift in range(1, members // 2 + 1):
-        other = jnp.concatenate([values[shift:], values[:shift]], axis=0)
-        side = side_of(values, other)
-        total += side
-        if shift < members // 2:
-            total -= jnp.concatenate([side[members - shift :], side[: members - shift]], axis=0)
-    gout[...] = (side_of(values, observed[None]) - total / (members - 1)).astype(jnp.bfloat16)
-
     def send_grad(i):
         to = lax.rem(me + i, members)
         return pltpu.make_async_remote_copy(
             src_ref=gout.at[to],
-            dst_ref=gext.at[me],
+            dst_ref=gext.at[jnp.where(scorer, place, 0)],
             send_sem=g_send.at[i],
             recv_sem=g_sem,
             device_id={"patch": me_p, "ens": to},
             device_id_type=MESH,
         )
 
-    lax.fori_loop(1, members, lambda i, c: (send_grad(i).start(), c)[1], 0)
-    pltpu.make_async_copy(gout.at[me], gext.at[me], g_sem).start()
+    @pl.when(scorer)
+    def _():
+        @pl.when(outside)
+        def _():
+            pin[...] = jnp.zeros(pin.shape, pin.dtype)
+            tin[...] = jnp.zeros(tin.shape, tin.dtype)
+
+        @pl.when(jnp.logical_not(outside))
+        def _():
+            with jax.named_scope("wait_pred"):
+                pltpu.make_async_copy(pin, pin, pin_sem).wait()
+                pltpu.make_async_copy(tin, tin, tin_sem).wait()
+
+        with jax.named_scope("score"):
+            for first in range(0, share, 16):
+                rows = slice(first, first + 16)
+                values = pin[:, rows].astype(jnp.float32)
+                observed = tin[rows].astype(jnp.float32)
+                total = jnp.zeros(values.shape, jnp.float32)
+                for shift in range(1, members // 2 + 1):
+                    other = jnp.concatenate([values[shift:], values[:shift]], axis=0)
+                    side = side_of(values, other)
+                    total += side
+                    if shift < members // 2:
+                        total -= jnp.concatenate(
+                            [side[members - shift :], side[: members - shift]], axis=0
+                        )
+                own_side = side_of(values, observed[None])
+                gout[:, rows] = (own_side - total / (members - 1)).astype(jnp.bfloat16)
+        with jax.named_scope("send_grad"):
+            pl.semaphore_wait(ready, members - 1)
+            lax.fori_loop(1, members, lambda i, c: (send_grad(i).start(), c)[1], 0)
+            pltpu.make_async_copy(
+                gout.at[me], gext.at[jnp.where(scorer, place, 0)], g_sem
+            ).start()
 
     load_w2.wait()
     w2c[0:512, 0:128] = w2v[0:512]
@@ -443,14 +470,18 @@
     each_target(lambda copy: copy.wait_send())
     each_halo(lambda copy: copy.wait_send())
     each_relay(lambda copy: copy.wait_send())
-    lax.fori_loop(1, members, lambda i, c: (send_grad(i).wait_send(), c)[1], 0)
+
+    @pl.when(scorer)
+    def _():
+        lax.fori_loop(1, members, lambda i, c: (send_grad(i).wait_send(), c)[1], 0)
 
 
 def per_device(pred, target, h1, w1, w2, neighbours, rotations):
     members = lax.axis_size("ens")
     patches = lax.axis_size("patch")
     rows, channels = h1.shape[1:]
-    share = 256 // members
+    scorers = members // 2
+    share = 256 // scorers
     relays = 8 if patches >= 64 else 1
     row_cuts = min(4, relays)
     anywhere = pl.BlockSpec(memory_space=pltpu.HBM)
@@ -467,7 +498,7 @@
             pltpu.VMEM((members, share, 128), bf16),
             pltpu.VMEM((share, 128), bf16),
             pltpu.VMEM((members, share, 128), bf16),
-            pltpu.VMEM((members, share, 128), bf16),
+            pltpu.VMEM((scorers, share, 128), bf16),
             pltpu.VMEM((channels, channels), bf16),
             pltpu.VMEM((channels, 128), bf16),
             pltpu.VMEM((channels, 256), bf16),
@@ -489,6 +520,7 @@
             dma((relays,)),
             dma(()),
             dma(()),
+            pltpu.SemaphoreType.REGULAR,
         ],
         compiler_params=pltpu.CompilerParams(
             collective_id=0, has_side_effects=True, vmem_limit_bytes=62 * 2**20

time: 50.9 us -> 40.7 us (0.80)
  the two profiles are of different devices: /device:TPU:7 before, /device:TPU:63 now
where the time goes in v2:
time: 40.7 us; the launch traced here: 40.5 us
  Pallas kernels  38.8 us (95%)
  local copies, waits for them, and re-layouts  1.67 us (4%)
    pallas_call x1, Pallas kernels, per_device(): pl.pallas_call(functools.partial(kernel, patches, members), out_shape=jax...  38.8 us
    unnamed x1, local copies, waits for them, and re-layouts  1.67 us

profile of v2, /device:TPU:63, one launch (start us, length us, event | category | flops | bytes accessed | tf_op | source)
XLA Modules:
  0.0 40.5 jit_solution(5185223570014698360)
XLA Ops:
  0.0 38.8 %mesh_backward.1 = bf16[128,1024]{1,0:T(8,128)(2,1)} custom-call(bf16[128,128]{1,0:T(8,128)(2,1)} %bitcast.7, bf16[128,128]{1,0:T(8,128)(2,1)} %target.1, bf16[128,1024]{1,0:T(8,128)(2,1)} %bitcast.6, bf16[1024,1024]{1,0:T(8,128)(2,1)} %w1.1, bf16[1024,128]{1,0:T(8,128)(2,1)} %w2.1, s32[6,1,256]{2,1,0:T(1,128)} %bitcast.8, s32[6,1,256]{2,1,0:T(1,128)} %bitcast.9), custom_call_target="tpu_custom_call" | custom-call | tf_op jit(solution)/shard_map/mesh_backward/pallas_call | solution.py:491
  38.8 1.7 %copy.9 = bf16[1,128,1024]{2,1,0:T(8,128)(2,1)} copy(bf16[1,128,1024]{2,1,0:T(8,128)(2,1)} %bitcast.5) | data formatting | bytes 524288

commit v3 on v2

--- a/solution.py
+++ b/solution.py
@@ -10,25 +10,28 @@
 K = 6
 H = 32
 MESH = pl.DeviceIdType.MESH
-RELAY_SIDE = "near"
+
+
+def relay_patches(side, half):
+    if half < 32:
+        return (half - 1 + half,) if side else (0,)
+    return (40, 63, 56, 39) if side else (23, 24, 7, 0)
 
 
 def relay_patch(side, index, half):
-    if half < 32:
-        return side * half + (half - 1 if side else 0)
-    row = index // 2
-    odd = lax.rem(index, 2)
-    return side * half + 8 * row + (2 + 5 * odd if side else 1 + 5 * odd)
+    patches = relay_patches(side, half)
+    patch = jnp.int32(patches[0])
+    for i, other in enumerate(patches):
+        patch = jnp.where(index == i, other, patch)
+    return patch
 
 
 def relay_job(side, patch, half):
-    if half < 32:
-        return patch == (2 * half - 1 if side else 0), 0
-    local = patch - side * half
-    column = lax.rem(local, 8)
-    odd, even = (7, 2) if side else (6, 1)
-    mine = (local >= 0) & (local < half) & ((column == odd) | (column == even))
-    return mine, 2 * (local // 8) + jnp.where(column == odd, 1, 0)
+    mine, index = patch < 0, jnp.int32(0)
+    for i, other in enumerate(relay_patches(side, half)):
+        mine = mine | (patch == other)
+        index = jnp.where(patch == other, i, index)
+    return mine, index
 
 
 def turn_table(turns):
@@ -88,6 +91,8 @@
     relay_recv,
     relay_send,
     ready,
+    cross,
+    c_send,
 ):
     me_p = lax.axis_index("patch")
     me = lax.axis_index("ens")
@@ -106,7 +111,12 @@
     low = scorer & (place < quarter)
     high = scorer & (place >= scorers - quarter)
     middle = (place >= quarter) & (place < scorers - quarter)
-    tail_side, head_side = (1, 0) if RELAY_SIDE == "far" else (0, 1)
+    tail_side, head_side = 0, 1
+    under, over = me_p == half - 1, me_p == half
+    has_left = (me_p > 0) & jnp.logical_not(over)
+    has_right = (me_p < last) & jnp.logical_not(under)
+    tail_scorer = under & middle & (place >= pieces)
+    head_scorer = over & middle & (place < pieces)
     tail_relay, tail_index = relay_job(tail_side, me_p, half)
     head_relay, head_index = relay_job(head_side, me_p, half)
 
@@ -132,37 +142,37 @@
     def _():
         lax.fori_loop(1, members, greet_own, 0)
 
-    @pl.when(low & (me_p > 0))
+    @pl.when(low & has_left)
     def _():
         lax.fori_loop(0, members, lambda i, c: (greet(me_p - 1, i), c)[1], 0)
 
-    @pl.when(high & (me_p < last))
+    @pl.when(high & has_right)
     def _():
         lax.fori_loop(0, members, lambda i, c: (greet(me_p + 1, i), c)[1], 0)
 
-    @pl.when((me_p > 0) & (me_p != half))
+    @pl.when(has_left)
     def _():
         greet(me_p - 1, me)
 
-    @pl.when((me_p < last) & (me_p != half - 1))
+    @pl.when(has_right)
     def _():
         greet(me_p + 1, me)
 
-    @pl.when(me_p == half)
-    def _():
-        lax.fori_loop(
-            0, relays, lambda i, c: (greet(relay_patch(tail_side, i, half), me), c)[1], 0
-        )
-
-    @pl.when(me_p == half - 1)
+    @pl.when(under)
     def _():
         lax.fori_loop(
             0, relays, lambda i, c: (greet(relay_patch(head_side, i, half), me), c)[1], 0
         )
+        lax.fori_loop(quarter, pieces, lambda i, c: (greet(half, base + i), c)[1], 0)
+
+    @pl.when(tail_scorer)
+    def _():
+        lax.fori_loop(0, members, lambda i, c: (greet(half, i), c)[1], 0)
 
     @pl.when(tail_relay)
     def _():
         greet(half - 1, me)
+        greet(half, me)
 
     @pl.when(head_relay)
     def _():
@@ -174,11 +184,12 @@
     partners = (
         scorers
         - count(scorer, 1)
-        + count(me_p < last, quarter)
-        + count(me_p > 0, quarter)
+        + count(has_right, quarter)
+        + count(has_left, quarter)
         + count(me_p < last, count(me_p == half - 1, relays - 1) + 1)
         + count(me_p > 0, count(me_p == half, relays - 1) + 1)
-        + count(tail_relay, 1)
+        + count(over, relays + quarter)
+        + count(head_scorer, members)
         + count(head_relay, 1)
     )
     pl.semaphore_wait(barrier, partners)
@@ -193,6 +204,20 @@
         return carry
 
     lax.fori_loop(0, scorers, tell, 0)
+
+    def tell_across(patch, ens):
+        pl.semaphore_signal(
+            cross, inc=1, device_id={"patch": patch, "ens": ens}, device_id_type=MESH
+        )
+
+    @pl.when(over)
+    def _():
+        lax.fori_loop(
+            0, relays, lambda i, c: (tell_across(relay_patch(tail_side, i, half), me), c)[1], 0
+        )
+        lax.fori_loop(
+            pieces, pieces + quarter, lambda i, c: (tell_across(half - 1, base + i), c)[1], 0
+        )
 
     def send_pred(piece, patch, to, slot):
         return pltpu.make_async_remote_copy(
@@ -209,11 +234,11 @@
             piece = lax.rem(me + i, pieces)
             upper = piece >= quarter
 
-            @pl.when(upper & (me_p < last))
+            @pl.when(upper & has_right)
             def _():
                 act(send_pred(piece, me_p + 1, piece - quarter, pieces + piece))
 
-            @pl.when(jnp.logical_not(upper) & (me_p > 0))
+            @pl.when(jnp.logical_not(upper) & has_left)
             def _():
                 act(send_pred(piece, me_p - 1, scorers - quarter + piece, pieces + piece))
 
@@ -238,11 +263,11 @@
         )
 
     def each_target(act):
-        @pl.when(low & (me_p < last))
+        @pl.when(low & has_right)
         def _():
             act(send_target((quarter + jnp.where(low, place, 0)) * share, me_p + 1))
 
-        @pl.when(high & (me_p > 0))
+        @pl.when(high & has_left)
         def _():
             act(send_target(jnp.where(high, place - (scorers - quarter), 0) * share, me_p - 1))
 
@@ -290,11 +315,11 @@
         )
 
     def each_halo(act):
-        @pl.when((me_p < last) & (me_p != half - 1))
+        @pl.when(has_right)
         def _():
             act(send_tail())
 
-        @pl.when((me_p > 0) & (me_p != half))
+        @pl.when(has_left)
         def _():
             act(send_head())
 
@@ -318,14 +343,11 @@
             device_id_type=MESH,
         )
 
-    def each_relay(act):
-        @pl.when(tail_relay)
-        def _():
-            act(onward(jnp.where(tail_relay, tail_index, 0), 0, half, 0))
-
-        @pl.when(head_relay)
-        def _():
-            act(onward(jnp.where(head_relay, head_index, 0), 192, half - 1, 1))
+    def forward_tail():
+        return onward(jnp.where(tail_relay, tail_index, 0), 0, half, 0)
+
+    def forward_head():
+        return onward(jnp.where(head_relay, head_index, 0), 192, half - 1, 1)
 
     for first in range(0, 256, 128):
         rows = slice(first, first + 128)
@@ -350,11 +372,10 @@
     def _():
         hext[192:256] = jnp.zeros((64, hext.shape[1]), hext.dtype)
 
-    @pl.when(tail_relay | head_relay)
+    @pl.when(head_relay)
     def _():
         pltpu.make_async_copy(relay, relay, relay_recv).wait()
-
-    each_relay(lambda copy: copy.start())
+        forward_head().start()
 
     outside = (low & (me_p == 0)) | (high & (me_p == last))
 
@@ -372,7 +393,30 @@
             device_id_type=MESH,
         )
 
-    @pl.when(scorer)
+    def send_across(i, patch, share_index):
+        to = lax.rem(me + i, members)
+        return pltpu.make_async_remote_copy(
+            src_ref=gout.at[to],
+            dst_ref=gext.at[share_index],
+            send_sem=c_send.at[i],
+            recv_sem=g_sem,
+            device_id={"patch": patch, "ens": to},
+            device_id_type=MESH,
+        )
+
+    def send_up(i):
+        return send_across(i, half, jnp.where(tail_scorer, place - pieces, 0))
+
+    def send_down(i):
+        return send_across(i, half - 1, jnp.where(head_scorer, place + pieces, 0))
+
+    idle = (low & over) | (high & under)
+
+    @pl.when(scorer & idle)
+    def _():
+        pl.semaphore_wait(ready, members - 1)
+
+    @pl.when(scorer & jnp.logical_not(idle))
     def _():
         @pl.when(outside)
         def _():
@@ -402,6 +446,11 @@
                 own_side = side_of(values, observed[None])
                 gout[:, rows] = (own_side - total / (members - 1)).astype(jnp.bfloat16)
         with jax.named_scope("send_grad"):
+
+            @pl.when(head_scorer)
+            def _():
+                lax.fori_loop(0, members, lambda i, c: (send_down(i).start(), c)[1], 0)
+
             pl.semaphore_wait(ready, members - 1)
             lax.fori_loop(1, members, lambda i, c: (send_grad(i).start(), c)[1], 0)
             pltpu.make_async_copy(
@@ -419,6 +468,11 @@
     @pl.when(me_p > 0)
     def _():
         pltpu.make_async_copy(hext.at[pl.ds(0, 64)], hext.at[pl.ds(0, 64)], h_recv.at[0]).wait()
+
+    @pl.when(tail_scorer)
+    def _():
+        pl.semaphore_wait(cross, members)
+        lax.fori_loop(0, members, lambda i, c: (send_up(i).start(), c)[1], 0)
 
     @pl.when(me_p < last)
     def _():
@@ -466,12 +520,33 @@
     out[:, :512] = (gmid[32:160, :512] + by_cos[:, :512] + by_sin[:, 512:]).astype(out.dtype)
     out[:, 512:] = (gmid[32:160, 512:] + by_cos[:, 512:] - by_sin[:, :512]).astype(out.dtype)
 
+    @pl.when(tail_relay)
+    def _():
+        pltpu.make_async_copy(relay, relay, relay_recv).wait()
+        pl.semaphore_wait(cross, 1)
+        forward_tail().start()
+
+    @pl.when(tail_relay)
+    def _():
+        forward_tail().wait_send()
+
+    @pl.when(head_relay)
+    def _():
+        forward_head().wait_send()
+
+    @pl.when(tail_scorer)
+    def _():
+        lax.fori_loop(0, members, lambda i, c: (send_up(i).wait_send(), c)[1], 0)
+
+    @pl.when(head_scorer)
+    def _():
+        lax.fori_loop(0, members, lambda i, c: (send_down(i).wait_send(), c)[1], 0)
+
     each_pred(lambda copy: copy.wait_send())
     each_target(lambda copy: copy.wait_send())
     each_halo(lambda copy: copy.wait_send())
-    each_relay(lambda copy: copy.wait_send())
-
-    @pl.when(scorer)
+
+    @pl.when(scorer & jnp.logical_not(idle))
     def _():
         lax.fori_loop(1, members, lambda i, c: (send_grad(i).wait_send(), c)[1], 0)
 
@@ -482,7 +557,7 @@
     rows, channels = h1.shape[1:]
     scorers = members // 2
     share = 256 // scorers
-    relays = 8 if patches >= 64 else 1
+    relays = 4 if patches >= 64 else 1
     row_cuts = min(4, relays)
     anywhere = pl.BlockSpec(memory_space=pltpu.HBM)
     vmem = pl.BlockSpec(memory_space=pltpu.VMEM)
@@ -521,6 +596,8 @@
             dma(()),
             dma(()),
             pltpu.SemaphoreType.REGULAR,
+            pltpu.SemaphoreType.REGULAR,
+            dma((members,)),
         ],
         compiler_params=pltpu.CompilerParams(
             collective_id=0, has_side_effects=True, vmem_limit_bytes=62 * 2**20

time: 40.7 us -> 38.1 us (0.936)
  Pallas kernels: 38.8 us -> 36.2 us
    pallas_call x1, Pallas kernels: 38.8 us -> 36.2 us  [per_device(): pl.pallas_call(functools.partial(kernel, patches, members), out_shape=jax...]
where the time goes in v3:
time: 38.1 us; the launch traced here: 37.9 us
  Pallas kernels  36.2 us (95%)
  local copies, waits for them, and re-layouts  1.67 us (4%)
    pallas_call x1, Pallas kernels, per_device(): pl.pallas_call(functools.partial(kernel, patches, members), out_shape=jax...  36.2 us
    unnamed x1, local copies, waits for them, and re-layouts  1.67 us

profile of v3, /device:TPU:63, one launch (start us, length us, event | category | flops | bytes accessed | tf_op | source)
XLA Modules:
  0.0 37.9 jit_solution(11364330653245334307)
XLA Ops:
  0.0 36.2 %mesh_backward.1 = bf16[128,1024]{1,0:T(8,128)(2,1)} custom-call(bf16[128,128]{1,0:T(8,128)(2,1)} %bitcast.7, bf16[128,128]{1,0:T(8,128)(2,1)} %target.1, bf16[128,1024]{1,0:T(8,128)(2,1)} %bitcast.6, bf16[1024,1024]{1,0:T(8,128)(2,1)} %w1.1, bf16[1024,128]{1,0:T(8,128)(2,1)} %w2.1, s32[6,1,256]{2,1,0:T(1,128)} %bitcast.8, s32[6,1,256]{2,1,0:T(1,128)} %bitcast.9), custom_call_target="tpu_custom_call" | custom-call | tf_op jit(solution)/shard_map/mesh_backward/pallas_call | solution.py:566
  36.2 1.7 %copy.9 = bf16[1,128,1024]{2,1,0:T(8,128)(2,1)} copy(bf16[1,128,1024]{2,1,0:T(8,128)(2,1)} %bitcast.5) | data formatting | bytes 524288

commit v4 on v3

--- a/solution.py
+++ b/solution.py
@@ -167,12 +167,12 @@
 
     @pl.when(tail_scorer)
     def _():
-        lax.fori_loop(0, members, lambda i, c: (greet(half, i), c)[1], 0)
+        lax.fori_loop(0, members, lambda i, c: (greet(half + 1, i), c)[1], 0)
 
     @pl.when(tail_relay)
     def _():
         greet(half - 1, me)
-        greet(half, me)
+        greet(half + 1, me)
 
     @pl.when(head_relay)
     def _():
@@ -188,36 +188,11 @@
         + count(has_left, quarter)
         + count(me_p < last, count(me_p == half - 1, relays - 1) + 1)
         + count(me_p > 0, count(me_p == half, relays - 1) + 1)
-        + count(over, relays + quarter)
+        + count(me_p == half + 1, relays + quarter)
         + count(head_scorer, members)
         + count(head_relay, 1)
     )
     pl.semaphore_wait(barrier, partners)
-
-    def tell(i, carry):
-        @pl.when(i != place)
-        def _():
-            pl.semaphore_signal(
-                ready, inc=1, device_id={"patch": me_p, "ens": base + i}, device_id_type=MESH
-            )
-
-        return carry
-
-    lax.fori_loop(0, scorers, tell, 0)
-
-    def tell_across(patch, ens):
-        pl.semaphore_signal(
-            cross, inc=1, device_id={"patch": patch, "ens": ens}, device_id_type=MESH
-        )
-
-    @pl.when(over)
-    def _():
-        lax.fori_loop(
-            0, relays, lambda i, c: (tell_across(relay_patch(tail_side, i, half), me), c)[1], 0
-        )
-        lax.fori_loop(
-            pieces, pieces + quarter, lambda i, c: (tell_across(half - 1, base + i), c)[1], 0
-        )
 
     def send_pred(piece, patch, to, slot):
         return pltpu.make_async_remote_copy(
@@ -251,6 +226,31 @@
         lax.fori_loop(0, pieces, across, 0)
 
     each_pred(lambda copy: copy.start())
+
+    def tell(i, carry):
+        @pl.when(i != place)
+        def _():
+            pl.semaphore_signal(
+                ready, inc=1, device_id={"patch": me_p, "ens": base + i}, device_id_type=MESH
+            )
+
+        return carry
+
+    lax.fori_loop(0, scorers, tell, 0)
+
+    def tell_across(patch, ens):
+        pl.semaphore_signal(
+            cross, inc=1, device_id={"patch": patch, "ens": ens}, device_id_type=MESH
+        )
+
+    @pl.when(me_p == half + 1)
+    def _():
+        lax.fori_loop(
+            0, relays, lambda i, c: (tell_across(relay_patch(tail_side, i, half), me), c)[1], 0
+        )
+        lax.fori_loop(
+            pieces, pieces + quarter, lambda i, c: (tell_across(half - 1, base + i), c)[1], 0
+        )
 
     def send_target(first, patch):
         return pltpu.make_async_remote_copy(
@@ -382,23 +382,31 @@
     def side_of(left, right):
         return jnp.where(left > right, 1.0, jnp.where(left < right, -1.0, 0.0))
 
-    def send_grad(i):
-        to = lax.rem(me + i, members)
+    def send_grad(to):
         return pltpu.make_async_remote_copy(
             src_ref=gout.at[to],
             dst_ref=gext.at[jnp.where(scorer, place, 0)],
-            send_sem=g_send.at[i],
+            send_sem=g_send.at[to],
             recv_sem=g_sem,
             device_id={"patch": me_p, "ens": to},
             device_id_type=MESH,
         )
 
-    def send_across(i, patch, share_index):
-        to = lax.rem(me + i, members)
+    def each_grad(act):
+        def one(to, carry):
+            @pl.when(to != me)
+            def _():
+                act(send_grad(to))
+
+            return carry
+
+        lax.fori_loop(0, members, one, 0)
+
+    def send_across(to, patch, share_index):
         return pltpu.make_async_remote_copy(
             src_ref=gout.at[to],
             dst_ref=gext.at[share_index],
-            send_sem=c_send.at[i],
+            send_sem=c_send.at[to],
             recv_sem=g_sem,
             device_id={"patch": patch, "ens": to},
             device_id_type=MESH,
@@ -452,7 +460,7 @@
                 lax.fori_loop(0, members, lambda i, c: (send_down(i).start(), c)[1], 0)
 
             pl.semaphore_wait(ready, members - 1)
-            lax.fori_loop(1, members, lambda i, c: (send_grad(i).start(), c)[1], 0)
+            each_grad(lambda copy: copy.start())
             pltpu.make_async_copy(
                 gout.at[me], gext.at[jnp.where(scorer, place, 0)], g_sem
             ).start()
@@ -548,7 +556,7 @@
 
     @pl.when(scorer & jnp.logical_not(idle))
     def _():
-        lax.fori_loop(1, members, lambda i, c: (send_grad(i).wait_send(), c)[1], 0)
+        each_grad(lambda copy: copy.wait_send())
 
 
 def per_device(pred, target, h1, w1, w2, neighbours, rotations):
@@ -565,7 +573,7 @@
     bf16 = jnp.bfloat16
     result = pl.pallas_call(
         functools.partial(kernel, patches, members),
-        out_shape=jax.ShapeDtypeStruct((rows, channels), bf16),
+        out_shape=pltpu.VMEM((rows, channels), bf16),
         in_specs=[anywhere, anywhere, anywhere, anywhere, anywhere, vmem, vmem],
         out_specs=vmem,
         scratch_shapes=[

time: 38.1 us -> 35.5 us (0.932)
  Pallas kernels: 36.2 us -> 34.6 us
  local copies, waits for them, and re-layouts: 1.67 us -> 0.71 us
    pallas_call x1, Pallas kernels: 36.2 us -> 34.6 us  [per_device(): pl.pallas_call(functools.partial(kernel, patches, members), out_shape=plt...]
    unnamed x1, local copies, waits for them, and re-layouts: 1.67 us -> 0.71 us
where the time goes in v4:
time: 35.5 us; the launch traced here: 35.3 us
  Pallas kernels  34.6 us (97%)
  local copies, waits for them, and re-layouts  0.71 us (2%)
    pallas_call x1, Pallas kernels, per_device(): pl.pallas_call(functools.partial(kernel, patches, members), out_shape=plt...  34.6 us

profile of v4, /device:TPU:63, one launch (start us, length us, event | category | flops | bytes accessed | tf_op | source)
XLA Modules:
  0.0 35.3 jit_solution(3411607862132762559)
XLA Ops:
  0.0 34.6 %mesh_backward.1 = bf16[128,1024]{1,0:T(8,128)(2,1)S(1)} custom-call(bf16[128,128]{1,0:T(8,128)(2,1)} %bitcast.7, bf16[128,128]{1,0:T(8,128)(2,1)} %target.1, bf16[128,1024]{1,0:T(8,128)(2,1)} %bitcast.6, bf16[1024,1024]{1,0:T(8,128)(2,1)} %w1.1, bf16[1024,128]{1,0:T(8,128)(2,1)} %w2.1, s32[6,1,256]{2,1,0:T(1,128)} %bitcast.8, s32[6,1,256]{2,1,0:T(1,128)} %bitcast.9), custom_call_target="tpu_custom_call" | custom-call | tf_op jit(solution)/shard_map/mesh_backward/pallas_call | solution.py:574
  34.6 0.7 %copy.9 = bf16[1,128,1024]{2,1,0:T(8,128)(2,1)} copy(bf16[1,128,1024]{2,1,0:T(8,128)(2,1)S(1)} %bitcast.5) | data formatting | bytes 524288

commit v5 on v4

--- a/solution.py
+++ b/solution.py
@@ -61,8 +61,8 @@
     h1,
     w1,
     w2,
-    links,
-    turns,
+    links_in,
+    turns_in,
     out,
     hext,
     pin,
@@ -93,6 +93,8 @@
     ready,
     cross,
     c_send,
+    links,
+    turns,
 ):
     me_p = lax.axis_index("patch")
     me = lax.axis_index("ens")
@@ -120,13 +122,6 @@
     tail_relay, tail_index = relay_job(tail_side, me_p, half)
     head_relay, head_index = relay_job(head_side, me_p, half)
 
-    own_h = pltpu.make_async_copy(h1, hext.at[pl.ds(64, 128)], load_sem.at[0])
-    own_h.start()
-    load_w2 = pltpu.make_async_copy(w2, w2v, load_sem.at[1])
-    load_w2.start()
-    load_w1 = pltpu.make_async_copy(w1, w1v, load_sem.at[2])
-    load_w1.start()
-
     barrier = pltpu.get_barrier_semaphore()
 
     def greet(patch, ens):
@@ -192,6 +187,17 @@
         + count(head_scorer, members)
         + count(head_relay, 1)
     )
+    own_h = pltpu.make_async_copy(h1, hext.at[pl.ds(64, 128)], load_sem.at[0])
+    own_h.start()
+    load_w2 = pltpu.make_async_copy(w2, w2v, load_sem.at[1])
+    load_w2.start()
+    load_w1 = pltpu.make_async_copy(w1, w1v, load_sem.at[2])
+    load_w1.start()
+    load_links = pltpu.make_async_copy(links_in, links, load_sem.at[3])
+    load_links.start()
+    load_turns = pltpu.make_async_copy(turns_in, turns, load_sem.at[4])
+    load_turns.start()
+
     pl.semaphore_wait(barrier, partners)
 
     def send_pred(piece, patch, to, slot):
@@ -349,6 +355,8 @@
     def forward_head():
         return onward(jnp.where(head_relay, head_index, 0), 192, half - 1, 1)
 
+    load_links.wait()
+    load_turns.wait()
     for first in range(0, 256, 128):
         rows = slice(first, first + 128)
         slots = lax.broadcasted_iota(jnp.int32, (128, 256), 0) + first
@@ -574,7 +582,7 @@
     result = pl.pallas_call(
         functools.partial(kernel, patches, members),
         out_shape=pltpu.VMEM((rows, channels), bf16),
-        in_specs=[anywhere, anywhere, anywhere, anywhere, anywhere, vmem, vmem],
+        in_specs=[anywhere] * 7,
         out_specs=vmem,
         scratch_shapes=[
             pltpu.VMEM((256, channels), bf16),
@@ -591,7 +599,7 @@
             pltpu.VMEM((192, channels), jnp.float32),
             pltpu.VMEM((256, channels), bf16),
             pltpu.VMEM((64 // row_cuts, channels * row_cuts // relays), bf16),
-            dma((3,)),
+            dma((5,)),
             dma(()),
             dma(()),
             dma((members,)),
@@ -606,6 +614,8 @@
             pltpu.SemaphoreType.REGULAR,
             pltpu.SemaphoreType.REGULAR,
             dma((members,)),
+            pltpu.VMEM((K, 1, 256), jnp.int32),
+            pltpu.VMEM((K, 1, 256), jnp.int32),
         ],
         compiler_params=pltpu.CompilerParams(
             collective_id=0, has_side_effects=True, vmem_limit_bytes=62 * 2**20

time: 35.5 us -> 34.9 us (0.983)
  Pallas kernels: 34.6 us -> 34 us
    pallas_call x1, Pallas kernels: 34.6 us -> 34 us  [per_device(): pl.pallas_call(functools.partial(kernel, patches, members), out_shape=plt...]
where the time goes in v5:
time: 34.9 us; the launch traced here: 34.7 us
  Pallas kernels  34 us (97%)
  local copies, waits for them, and re-layouts  0.71 us (2%)
    pallas_call x1, Pallas kernels, per_device(): pl.pallas_call(functools.partial(kernel, patches, members), out_shape=plt...  34 us
    unnamed x1, local copies, waits for them, and re-layouts  0.71 us

profile of v5, /device:TPU:63, one launch (start us, length us, event | category | flops | bytes accessed | tf_op | source)
XLA Modules:
  0.0 34.7 jit_solution(475389707697357050)
XLA Ops:
  0.0 34.0 %mesh_backward.1 = bf16[128,1024]{1,0:T(8,128)(2,1)S(1)} custom-call(bf16[128,128]{1,0:T(8,128)(2,1)} %bitcast.7, bf16[128,128]{1,0:T(8,128)(2,1)} %target.1, bf16[128,1024]{1,0:T(8,128)(2,1)} %bitcast.6, bf16[1024,1024]{1,0:T(8,128)(2,1)} %w1.1, bf16[1024,128]{1,0:T(8,128)(2,1)} %w2.1, s32[6,1,256]{2,1,0:T(1,128)} %bitcast.8, s32[6,1,256]{2,1,0:T(1,128)} %bitcast.9), custom_call_target="tpu_custom_call" | custom-call | tf_op jit(solution)/shard_map/mesh_backward/pallas_call | solution.py:582
  34.0 0.7 %copy.9 = bf16[1,128,1024]{2,1,0:T(8,128)(2,1)} copy(bf16[1,128,1024]{2,1,0:T(8,128)(2,1)S(1)} %bitcast.5) | data formatting | bytes 524288
